TPU v7x, 512 devices: a whole 4x4x16 slice. The times are simulated.
512 devices in a mesh: group: 8 (over x, core), dev: 64 (over z, y).
Axes of the slice: x: 4, y: 4, z: 16, core: 2. Of those that a mesh axis runs over, the one named last changes fastest.
Arguments:
- cam_jac: float32 [2, 9, 8, 262144], P(None, None, None, ('group', 'dev')), may hold values from -6 to 6
- lm_jac: float32 [2, 3, 8, 262144], P(None, None, None, ('group', 'dev')), may hold values from -6 to 6
- resid: float32 [2, 8, 262144], P(None, None, ('group', 'dev')), may hold values from -6 to 6
- cam_index: int32 [8, 262144], P(None, ('group', 'dev')), may hold values from 0 to 8191
Outputs:
- camera_step: float32 [9, 8192], P(None, 'dev')
- camera_residual: float32 [9, 8192], P(None, 'dev')
- landmark_step: float32 [3, 262144], P(None, ('group', 'dev'))
Inputs may be any that keep to these rules, and one draw needn't show every extreme that they name: `cam_index`: every observation names one of the 8192 cameras.
All inputs are finite; a program needn't handle non-finite values.
Results may differ from a plain program's by a relative error of at most 0.0003.
Values sent between devices are 32-bit elements; how exact they have to be, the bound alone decides.
A program may use at most 64 MiB of HBM per device.

v0:
```python
import jax
import jax.numpy as jnp
from jax import lax
from jax.sharding import PartitionSpec as P

CAM_DEV = 128
ITERS = 2
DAMPING = 1.0


def landmark_inverse(lm_jac):

    def entry(first, second):
        return jnp.sum(lm_jac[:, first] * lm_jac[:, second], axis=(0, 1))

    w_00 = entry(0, 0) + DAMPING
    w_11 = entry(1, 1) + DAMPING
    w_22 = entry(2, 2) + DAMPING
    w_01 = entry(0, 1)
    w_02 = entry(0, 2)
    w_12 = entry(1, 2)
    cof_00 = w_11 * w_22 - w_12 * w_12
    cof_01 = w_02 * w_12 - w_01 * w_22
    cof_02 = w_01 * w_12 - w_02 * w_11
    cof_11 = w_00 * w_22 - w_02 * w_02
    cof_12 = w_01 * w_02 - w_00 * w_12
    cof_22 = w_00 * w_11 - w_01 * w_01
    determinant = w_00 * cof_00 + w_01 * cof_01 + w_02 * cof_02
    rows = [
        jnp.stack([cof_00, cof_01, cof_02]),
        jnp.stack([cof_01, cof_11, cof_12]),
        jnp.stack([cof_02, cof_12, cof_22]),
    ]
    return jnp.stack(rows) / determinant[None, None]


def apply_inverse(inverse, vector):
    return jnp.sum(inverse * vector[None], axis=1)


def landmark_side(lm_jac, values):
    return jnp.sum(lm_jac * values[:, None], axis=(0, 2))


def back_project(lm_jac, landmark):
    return jnp.sum(lm_jac * landmark[None, :, None, :], axis=1)


def camera_apply(cam_jac, cam_values):
    return jnp.sum(cam_jac * cam_values[None], axis=1)


def camera_transpose(cam_jac, errors):
    return jnp.sum(cam_jac * errors[:, None], axis=0)


def to_cameras(values, cam_index, total_cams):
    flat_index = cam_index.reshape(-1)
    width = values.shape[0]

    def one_row(column):
        return jax.ops.segment_sum(column, flat_index, num_segments=total_cams)

    return jax.vmap(one_row)(values.reshape(width, -1))


def schur_obs(cam_jac, lm_jac, inverse, cam_values):
    applied = camera_apply(cam_jac, cam_values)
    landmark = apply_inverse(inverse, landmark_side(lm_jac, applied))
    return camera_transpose(cam_jac, applied - back_project(lm_jac, landmark))


def gather_cameras(tile):
    return lax.all_gather(tile, "dev", axis=1, tiled=True)


def reduce_cameras(terms):
    totals = lax.psum(terms, ("group", "dev"))
    width = terms.shape[1] // lax.axis_size("dev")
    return lax.dynamic_slice_in_dim(totals, lax.axis_index("dev") * width, width, 1)


def inner_product(left, right):
    return lax.psum(jnp.sum(left * right), "dev")


def body(cam_jac, lm_jac, resid, cam_index):
    total_cams = CAM_DEV * lax.axis_size("dev")
    inverse = landmark_inverse(lm_jac)
    land_rhs = apply_inverse(inverse, landmark_side(lm_jac, resid))
    errors = resid - back_project(lm_jac, land_rhs)
    stacked = jnp.concatenate(
        [camera_transpose(cam_jac, errors), jnp.sum(cam_jac * cam_jac, axis=0)], axis=0
    )
    summed = reduce_cameras(to_cameras(stacked, cam_index, total_cams))
    gradient = summed[:9]
    diagonal = summed[9:] + DAMPING
    residual = gradient
    precond = residual / diagonal
    direction = precond
    rz_now = inner_product(residual, precond)
    solution = jnp.zeros_like(gradient)
    for iteration in range(ITERS):
        whole = gather_cameras(direction)
        cam_values = jnp.take(whole, cam_index, axis=1)
        terms = to_cameras(schur_obs(cam_jac, lm_jac, inverse, cam_values), cam_index, total_cams)
        image = reduce_cameras(terms) + DAMPING * direction
        alpha = rz_now / inner_product(direction, image)
        solution = solution + alpha * direction
        residual = residual - alpha * image
        if iteration + 1 < ITERS:
            precond = residual / diagonal
            rz_next = inner_product(residual, precond)
            direction = precond + rz_next / rz_now * direction
            rz_now = rz_next
    whole_step = gather_cameras(solution)
    cam_obs = camera_apply(cam_jac, jnp.take(whole_step, cam_index, axis=1))
    landmark_step = land_rhs - apply_inverse(inverse, landmark_side(lm_jac, cam_obs))
    return (solution, residual, landmark_step)


def solution(mesh):
    in_specs = (
        P(None, None, None, ("group", "dev")),
        P(None, None, None, ("group", "dev")),
        P(None, None, ("group", "dev")),
        P(None, ("group", "dev")),
    )
    out_specs = (P(None, "dev"), P(None, "dev"), P(None, ("group", "dev")))
    return jax.shard_map(body, mesh=mesh, in_specs=in_specs, out_specs=out_specs, check_vma=False)
```

profile of v0, /device:TPU:8, one launch (start us, length us, event | category | flops | bytes accessed | tf_op | source)
XLA Modules:
  0.0 2390.0 jit_solution(14837299796872105308)
XLA Ops:
  7.2 0.8 multiply_reduce_fusion.22
  8.0 0.9 multiply_reduce_fusion.13
  9.0 0.7 copy.31
  9.8 0.9 multiply_reduce_fusion.12
  10.7 0.8 sub.128
  11.5 1.0 multiply_reduce_fusion.6
  13.2 24.5 %scatter_custom_fusion = f32[18,8192]{0,1:T(8,128)} fusion(s32[4096]{0:T(1024)S(1)} %bitcast.43, f32[4096,18]{1,0:T(8,128)S(1)} %bitcast.38, f32[]{:T(128)} %constant.14.clone.1), kind=kCustom, calls=%fused_computation.13 | custom fusion | flops 73728 | bytes 589828 | tf_op jit(solution)/shard_map/vmap()/scatter-add | solution.py:62
  37.9 494.2 %all-reduce.5.cloned.1.call-done = f32[18,8192]{0,1:T(8,128)} async-done(((f32[18,8192]{0,1:T(8,128)}), f32[18,8192]{0,1:T(8,128)}) %all-reduce.5.cloned.1.call-update) | async-done | bytes 589840 | tf_op jit(solution)/shard_map/psum | solution.py:78
  532.1 1.0 fusion.7
  533.1 111.9 %all_gather.9 = f32[9,8192]{0,1:T(8,128)} all-gather(f32[9,128]{0,1:T(8,128)S(1)} %fusion.7), channel_id=1, replica_groups=mesh['group'=8,'dev'=64] {'dev'}, dimensions={1}, use_global_device_ids=true | all-gather | bytes 299520 | tf_op jit(solution)/shard_map/all_gather | solution.py:74
  645.0 16.3 gather_fusion
  661.3 1.9 select_bitcast_fusion.2
  664.8 24.5 %scatter_custom_fusion.1 = f32[9,8192]{0,1:T(8,128)} fusion(s32[4096]{0:T(1024)S(1)} %bitcast.44, f32[4096,9]{1,0:T(8,128)S(1)} %bitcast.40, f32[]{:T(128)} %constant.14.clone.1), kind=kCustom, calls=%fused_computation.11 | custom fusion | flops 36864 | bytes 294916 | tf_op jit(solution)/shard_map/vmap()/scatter-add | solution.py:62
  689.4 488.0 %all-reduce.7.cloned.1.call-done = f32[9,8192]{0,1:T(8,128)} async-done(((f32[9,8192]{0,1:T(8,128)}), f32[9,8192]{0,1:T(8,128)}) %all-reduce.7.cloned.1.call-update) | async-done | bytes 294928 | tf_op jit(solution)/shard_map/psum | solution.py:78
  1177.4 1.6 multiply_reduce_fusion.16
  1179.0 139.5 %all-reduce = (f32[]{:T(128)}, f32[]{:T(128)}) all-reduce(f32[]{:T(128)} %get-tuple-element.22, f32[]{:T(128)} %get-tuple-element.21), channel_id=1, replica_groups=mesh['group'=8,'dev'=64] {'dev'}, use_global_device_ids=true, to_apply=%region_14.0 | all-reduce | flops 2 | bytes 16 | tf_op jit(solution)/shard_map/psum | solution.py:84
  1319.8 1.6 multiply_reduce_fusion.15
  1321.4 140.7 %psum.53 = f32[]{:T(128)} all-reduce(f32[]{:T(128)} %get-tuple-element.25), channel_id=1, replica_groups=mesh['group'=8,'dev'=64] {'dev'}, use_global_device_ids=true, to_apply=%region_25.27 | all-reduce | flops 1 | bytes 8 | tf_op jit(solution)/shard_map/psum | solution.py:84
  1463.5 1.0 multiply_add_fusion.1
  1464.5 110.5 %all_gather.10 = f32[9,8192]{0,1:T(8,128)} all-gather(f32[9,128]{0,1:T(8,128)S(1)} %multiply_add_fusion.1), channel_id=1, replica_groups=mesh['group'=8,'dev'=64] {'dev'}, dimensions={1}, use_global_device_ids=true | all-gather | bytes 299520 | tf_op jit(solution)/shard_map/all_gather | solution.py:74
  1575.0 16.3 gather_fusion.1
  1591.2 1.9 select_bitcast_fusion.1
  1594.6 24.5 %scatter_custom_fusion.2 = f32[9,8192]{0,1:T(8,128)} fusion(s32[4096]{0:T(1024)S(1)} %bitcast.45, f32[4096,9]{1,0:T(8,128)S(1)} %bitcast.39, f32[]{:T(128)} %constant.14.clone.1), kind=kCustom, calls=%fused_computation.9 | custom fusion | flops 36864 | bytes 294916 | tf_op jit(solution)/shard_map/vmap()/scatter-add | solution.py:62
  1619.2 488.2 %all-reduce.9.cloned.1.call-done = f32[9,8192]{0,1:T(8,128)} async-done(((f32[9,8192]{0,1:T(8,128)}), f32[9,8192]{0,1:T(8,128)}) %all-reduce.9.cloned.1.call-update) | async-done | bytes 294928 | tf_op jit(solution)/shard_map/psum | solution.py:78
  2107.4 1.5 multiply_reduce_fusion.14
  2108.9 139.4 %psum.55 = f32[]{:T(128)} all-reduce(f32[]{:T(128)} %multiply_reduce_fusion.14), channel_id=1, replica_groups=mesh['group'=8,'dev'=64] {'dev'}, use_global_device_ids=true, to_apply=%region_34.36 | all-reduce | flops 1 | bytes 8 | tf_op jit(solution)/shard_map/psum | solution.py:84
  2249.7 1.0 multiply_subtract_fusion
  2250.7 0.7 copy.26
  2251.4 111.8 %all_gather.11 = f32[9,8192]{0,1:T(8,128)} all-gather(f32[9,128]{0,1:T(8,128)S(1)} %get-tuple-element.34), channel_id=1, replica_groups=mesh['group'=8,'dev'=64] {'dev'}, dimensions={1}, use_global_device_ids=true | all-gather | bytes 299520 | tf_op jit(solution)/shard_map/all_gather | solution.py:74
  2363.2 0.7 copy.27
  2363.9 16.3 gather_fusion.2
  2380.2 1.9 select_bitcast_fusion
  (42 shorter events, 5.1 us)
Async XLA Ops:
  7.2 524.9 %all-reduce.5.cloned.1.call-start = ((), (), s32[]{:S(2)}) async-start(), calls=%async_computation | async-start | bytes 8388608 | tf_op jit(solution)/shard_map/psum | solution.py:78
  13.2 24.6 %copy-start.2 = (s32[8,512]{1,0:T(8,128)S(1)}, s32[8,512]{1,0:T(8,128)}, u32[]{:S(2)}) copy-start(s32[8,512]{1,0:T(8,128)} %param.9) | copy-start | bytes 49156
  37.8 1139.6 %all-reduce.7.cloned.1.call-start = ((), (), s32[]{:S(2)}) async-start(), calls=%async_computation.1 | async-start | bytes 8388608 | tf_op jit(solution)/shard_map/psum | solution.py:78
  645.0 18.9 copy-start
  645.0 19.0 copy-start.1
  689.3 1418.1 %all-reduce.9.cloned.1.call-start = ((), (), s32[]{:S(2)}) async-start(), calls=%async_computation.2 | async-start | bytes 8388608 | tf_op jit(solution)/shard_map/psum | solution.py:78
Sparse Core Ops, SparseCore 0:
  37.9 494.1 all-reduce.4
  689.4 487.8 all-reduce.6
  1619.3 488.0 all-reduce.8
where the time goes:
time: 2390 us
  waiting for transfers between devices  1470 us (62%)
  blocking collectives  754 us (32%)
  other arithmetic  92.8 us (4%)
  local copies, waits for them, and re-layouts  54.8 us (2%)
    psum x3, waiting for transfers between devices, reduce_cameras(): totals = lax.psum(terms, ('group', 'dev'))  1470 us
    psum x3, blocking collectives, inner_product(): return lax.psum(jnp.sum(left * right), 'dev')  420 us
    all_gather x3, blocking collectives, gather_cameras(): return lax.all_gather(tile, 'dev', axis=1, tiled=True)  334 us
    scatter-add x3, other arithmetic, one_row(): return jax.ops.segment_sum(column, flat_index, num_segments=total_cams)  73.6 us
  transfers between devices with their start and end apart: 3, of which 3 were waited for; matrix products, arithmetic and copies ran while one was open for 0% of the time, Pallas kernels for 0%

commit v1 on v0

--- a/solution.py
+++ b/solution.py
@@ -2,10 +2,23 @@
 import jax.numpy as jnp
 from jax import lax
 from jax.sharding import PartitionSpec as P
+from jax.lax import axis_index, ppermute, psum
 
 CAM_DEV = 128
 ITERS = 2
 DAMPING = 1.0
+
+
+def shape_cube(local_array, chip_axis, in_dim):
+    s_next, prior = (psum(1, chip_axis), axis_index(chip_axis))
+    heard, local_out = (local_array, 1)
+    while local_out < s_next:
+        y = ppermute(heard, chip_axis, tuple(((j, j ^ local_out) for j in range(s_next))))
+        reached = jnp.concatenate([heard, y], axis=in_dim)
+        clean = jnp.concatenate([y, heard], axis=in_dim)
+        heard = jnp.where(prior & local_out == 0, reached, clean)
+        local_out = 2 * local_out
+    return heard
 
 
 def landmark_inverse(lm_jac):
@@ -71,7 +84,7 @@
 
 
 def gather_cameras(tile):
-    return lax.all_gather(tile, "dev", axis=1, tiled=True)
+    return shape_cube(tile, "dev", 1)
 
 
 def reduce_cameras(terms):

time: 2390 us -> 2210 us (0.925)
  the two profiles are of different devices: /device:TPU:8 before, /device:TPU:6 now
where the time goes in v1:
time: 2210 us
  waiting for transfers between devices  1520 us (69%)
  blocking collectives  420 us (19%)
  other arithmetic  106 us (5%)
  local copies, waits for them, and re-layouts  79.9 us (4%)
  starting transfers between devices  70.9 us (3%)
    psum x3, waiting for transfers between devices, reduce_cameras(): totals = lax.psum(terms, ('group', 'dev'))  1390 us
    psum x3, blocking collectives, inner_product(): return lax.psum(jnp.sum(left * right), 'dev')  420 us
    ppermute x18, waiting for transfers between devices, shape_cube(): ppermute(heard, chip_axis, tuple(((j, j ^ local_out) for j in range(s_nex...  126 us
    scatter-add x3, other arithmetic, one_row(): return jax.ops.segment_sum(column, flat_index, num_segments=total_cams)  73.5 us
    ppermute x18, starting transfers between devices, shape_cube(): ppermute(heard, chip_axis, tuple(((j, j ^ local_out) for j in range(s_nex...  70.8 us
  transfers between devices with their start and end apart: 21, of which 21 were waited for; matrix products, arithmetic and copies ran while one was open for 0% of the time, Pallas kernels for 0%

profile of v1, /device:TPU:6, one launch (start us, length us, event | category | flops | bytes accessed | tf_op | source)
XLA Modules:
  0.0 2211.8 jit_solution(1200947291117172686)
XLA Ops:
  13.2 24.5 %scatter_custom_fusion = f32[18,8192]{0,1:T(8,128)} fusion(s32[4096]{0:T(1024)S(1)} %bitcast.43, f32[4096,18]{1,0:T(8,128)S(1)} %bitcast.38, f32[]{:T(128)} %constant.20.clone.1), kind=kCustom, calls=%fused_computation.13 | custom fusion | flops 73728 | bytes 589828 | tf_op jit(solution)/shard_map/vmap()/scatter-add | solution.py:75
  41.4 473.0 %all-reduce.5.cloned.1.call-done = f32[18,8192]{1,0:T(8,128)} async-done(((f32[18,8192]{1,0:T(8,128)}), f32[18,8192]{1,0:T(8,128)}) %all-reduce.5.cloned.1.call-update) | async-done | bytes 589840 | tf_op jit(solution)/shard_map/psum | solution.py:91
  535.7 5.2 collective-permute-done.3
  540.9 5.3 collective-permute-start.4
  546.2 10.0 collective-permute-done.4
  556.2 9.1 collective-permute-start.5
  565.4 21.7 collective-permute-done.5
  592.4 4.6 broadcast_select_fusion.2
  597.0 16.3 gather_fusion
  616.7 24.5 %scatter_custom_fusion.1 = f32[9,8192]{0,1:T(8,128)} fusion(s32[4096]{0:T(1024)S(1)} %bitcast.44, f32[4096,9]{1,0:T(8,128)S(1)} %bitcast.40, f32[]{:T(128)} %constant.20.clone.1), kind=kCustom, calls=%fused_computation.11 | custom fusion | flops 36864 | bytes 294916 | tf_op jit(solution)/shard_map/vmap()/scatter-add | solution.py:75
  644.9 454.8 %all-reduce.7.cloned.1.call-done = f32[9,8192]{1,0:T(8,128)} async-done(((f32[9,8192]{1,0:T(8,128)}), f32[9,8192]{1,0:T(8,128)}) %all-reduce.7.cloned.1.call-update) | async-done | bytes 294928 | tf_op jit(solution)/shard_map/psum | solution.py:91
  1101.2 140.5 %all-reduce = (f32[]{:T(128)}, f32[]{:T(128)}) all-reduce(f32[]{:T(128)} %get-tuple-element.22, f32[]{:T(128)} %get-tuple-element.21), channel_id=1, replica_groups=mesh['group'=8,'dev'=64] {'dev'}, use_global_device_ids=true, to_apply=%region_14.0 | all-reduce | flops 2 | bytes 16 | tf_op jit(solution)/shard_map/psum | solution.py:97
  1244.4 139.4 %psum.53 = f32[]{:T(128)} all-reduce(f32[]{:T(128)} %get-tuple-element.25), channel_id=1, replica_groups=mesh['group'=8,'dev'=64] {'dev'}, use_global_device_ids=true, to_apply=%region_25.27 | all-reduce | flops 1 | bytes 8 | tf_op jit(solution)/shard_map/psum | solution.py:97
  1393.5 5.2 collective-permute-done.7
  1406.5 5.3 collective-permute-done.9
  1411.8 6.3 collective-permute-start.10
  1418.1 7.9 collective-permute-done.10
  1426.1 9.1 collective-permute-start.11
  1435.2 8.1 collective-permute-done.11
  1448.7 4.6 broadcast_select_fusion.1
  1453.3 16.3 gather_fusion.1
  1472.9 24.5 %scatter_custom_fusion.2 = f32[9,8192]{0,1:T(8,128)} fusion(s32[4096]{0:T(1024)S(1)} %bitcast.45, f32[4096,9]{1,0:T(8,128)S(1)} %bitcast.39, f32[]{:T(128)} %constant.20.clone.1), kind=kCustom, calls=%fused_computation.9 | custom fusion | flops 36864 | bytes 294916 | tf_op jit(solution)/shard_map/vmap()/scatter-add | solution.py:75
  1501.0 461.8 %all-reduce.9.cloned.1.call-done = f32[9,8192]{1,0:T(8,128)} async-done(((f32[9,8192]{1,0:T(8,128)}), f32[9,8192]{1,0:T(8,128)}) %all-reduce.9.cloned.1.call-update) | async-done | bytes 294928 | tf_op jit(solution)/shard_map/psum | solution.py:91
  1964.1 140.4 %psum.55 = f32[]{:T(128)} all-reduce(f32[]{:T(128)} %multiply_reduce_fusion.24), channel_id=1, replica_groups=mesh['group'=8,'dev'=64] {'dev'}, use_global_device_ids=true, to_apply=%region_34.36 | all-reduce | flops 1 | bytes 8 | tf_op jit(solution)/shard_map/psum | solution.py:97
  2114.8 5.2 collective-permute-done.13
  2121.9 5.7 collective-permute-done.14
  2129.5 6.4 collective-permute-done.15
  2139.1 11.6 collective-permute-done.16
  2150.7 9.7 collective-permute-start.17
  2160.4 15.3 collective-permute-done.17
  2181.1 4.6 broadcast_select_fusion
  2185.7 16.3 gather_fusion.2
  (105 shorter events, 100.3 us)
Async XLA Ops:
  7.2 507.2 %all-reduce.5.cloned.1.call-start = ((), (), s32[]{:S(2)}) async-start(), calls=%async_computation | async-start | bytes 1572864 | tf_op jit(solution)/shard_map/psum | solution.py:91
  13.2 522.5 %copy-start.2 = (s32[8,512]{1,0:T(8,128)S(1)}, s32[8,512]{1,0:T(8,128)}, u32[]{:S(2)}) copy-start(s32[8,512]{1,0:T(8,128)} %param.9) | copy-start | bytes 49156
  41.3 1058.4 %all-reduce.7.cloned.1.call-start = ((), (), s32[]{:S(2)}) async-start(), calls=%async_computation.1 | async-start | bytes 1048576 | tf_op jit(solution)/shard_map/psum | solution.py:91
  515.2 5.5 collective-permute-start
  520.8 7.1 collective-permute-start.1
  527.9 5.8 collective-permute-start.2
  533.7 7.2 collective-permute-start.3
  540.9 15.3 collective-permute-start.4
  556.2 30.8 %collective-permute-start.5 = (f32[9,4096]{1,0:T(8,128)S(1)}, f32[9,4096]{1,0:T(8,128)S(1)}, u32[]{:S(2)}, u32[]{:S(2)}) collective-permute-start(f32[9,4096]{1,0:T(8,128)S(1)} %maximum_select_fusion), channel_id=1, source_target_pairs={{0,32},{1,33},{2,34},{3,35},{4,36},{5,37},{6,38},{7,39},{8,40},{9,... | collective-permute-start | bytes 442376 | tf_op jit(solution)/shard_map/ppermute | solution.py:16
  597.0 18.9 copy-start
  597.0 18.9 copy-start.1
  644.8 1318.0 %all-reduce.9.cloned.1.call-start = ((), (), s32[]{:S(2)}) async-start(), calls=%async_computation.2 | async-start | bytes 1048576 | tf_op jit(solution)/shard_map/psum | solution.py:91
  1386.1 5.5 collective-permute-start.6
  1391.6 7.1 collective-permute-start.7
  1398.7 5.8 collective-permute-start.8
  1404.6 7.2 collective-permute-start.9
  1411.8 14.3 collective-permute-start.10
  1426.1 17.2 collective-permute-start.11
  2107.3 73.8 %copy-start.3 = (f32[9,128]{1,0:T(8,128)}, f32[9,128]{1,0:T(8,128)S(1)}, u32[]{:S(2)}) copy-start(f32[9,128]{1,0:T(8,128)S(1)} %get-tuple-element.40) | copy-start | bytes 13828
  2107.3 5.5 collective-permute-start.12
  2112.8 7.1 collective-permute-start.13
  2120.0 7.6 collective-permute-start.14
  2127.6 8.3 collective-permute-start.15
  2135.9 14.8 collective-permute-start.16
  2150.7 25.0 %collective-permute-start.17 = (f32[9,4096]{1,0:T(8,128)S(1)}, f32[9,4096]{1,0:T(8,128)S(1)}, u32[]{:S(2)}, u32[]{:S(2)}) collective-permute-start(f32[9,4096]{1,0:T(8,128)S(1)} %maximum_select_fusion.2), channel_id=1, source_target_pairs={{0,32},{1,33},{2,34},{3,35},{4,36},{5,37},{6,38},{7,39},{8,40},{9,... | collective-permute-start | bytes 442376 | tf_op jit(solution)/shard_map/ppermute | solution.py:16
Sparse Core Ops, SparseCore 0:
  41.4 472.9 all-reduce.4
  644.9 454.7 all-reduce.6
  1501.1 461.6 all-reduce.8
